TPU v7x, 32 devices: a whole 2x2x4 slice. The times are simulated.
32 devices in a mesh: grp: 2 (over x), col: 8 (over z, y), row: 2 (over core).
Axes of the slice: x: 2, y: 2, z: 4, core: 2. Of those that a mesh axis runs over, the one named last changes fastest.
Arguments:
- grad_out: bfloat16 [384, 8192], P('grp', 'col'), parts along dimension 0, may hold values from -6 to 6
- hidden: bfloat16 [384, 26624], P(('grp', 'col'), 'row'), parts along dimension 0, may hold values from -6 to 6
- weight: bfloat16 [8192, 26624], P('col', 'row'), may hold values from -0.0625 to 0.0625
- proj_in: bfloat16 [64, 26624], P(None, 'row'), may hold values from -0.0390625 to 0.0390625
- proj_out: bfloat16 [64, 8192], P(None, 'col'), may hold values from -0.0625 to 0.0625
- doc_len: int32 [32], P('grp'), parts along dimension 0, may hold values from 1 to 48, 192 in all
Outputs:
- input_grad: bfloat16 [384, 26624], P(('grp', 'col'), 'row'), parts along dimension 0
- doc_grads: float32 [32, 64, 64], P('grp'), parts along dimension 0
There are 2 independent parts, one for each index of `grp`. A program takes and returns all parts, laid end to end along the dimension named above; an argument that names none is the same for every part. Nothing has to cross between parts.
Inputs may be any that keep to these rules, and one draw needn't show every extreme that they name: doc_len sums to 192; its largest entry is exactly 48.
All inputs are finite; a program needn't handle non-finite values.
Results may differ from a plain program's by a relative error of at most 0.014.
Values may be sent and summed in bfloat16 or wider, within the bound.
A program may use at most 128 MiB of HBM per device.

v0:
```python
import jax
import jax.numpy as jnp
from jax import lax
from jax.sharding import PartitionSpec as P


def member_table(doc_len, first, count):
    starts = jnp.cumsum(doc_len) - doc_len
    places = first + jnp.arange(count, dtype=jnp.int32)
    member = (places[None, :] >= starts[:, None]) & (places[None, :] < (starts + doc_len)[:, None])
    return member.astype(jnp.float32)


def doc_terms(doc_len, first, out_part, in_part):
    member = member_table(doc_len, first, out_part.shape[0])
    weighted = member[:, :, None] * out_part.astype(jnp.float32)[None, :, :]
    return jnp.einsum("sti,tj->sij", weighted, in_part.astype(jnp.float32))


def local(grad_out, hidden, weight, proj_in, proj_out, doc_len):
    contract = (((1,), (1,)), ((), ()))
    local_rows = hidden.shape[0]
    local_in = lax.dot_general(hidden, proj_in, contract, preferred_element_type=jnp.float32)
    in_sketch = lax.psum(local_in, "row").astype(jnp.bfloat16)
    input_grad = lax.psum_scatter(
        jnp.dot(grad_out, weight, preferred_element_type=jnp.float32).astype(jnp.bfloat16),
        "col",
        scatter_dimension=0,
        tiled=True,
    )
    local_out = lax.dot_general(grad_out, proj_out, contract, preferred_element_type=jnp.float32)
    out_sketch = lax.psum_scatter(
        local_out.astype(jnp.bfloat16), "col", scatter_dimension=0, tiled=True
    )
    first = lax.axis_index("col") * local_rows
    local_docs = doc_terms(doc_len, first, out_sketch, in_sketch)
    doc_grads = lax.psum(local_docs.astype(jnp.bfloat16), "col").astype(jnp.float32)
    return (input_grad, doc_grads)


def solution(mesh):
    in_specs = (
        P("grp", "col"),
        P(("grp", "col"), "row"),
        P("col", "row"),
        P(None, "row"),
        P(None, "col"),
        P("grp"),
    )
    out_specs = (P(("grp", "col"), "row"), P("grp", None, None))
    return jax.shard_map(local, mesh=mesh, in_specs=in_specs, out_specs=out_specs, check_vma=False)
```

profile of v0, /device:TPU:0, one launch (start us, length us, event | category | flops | bytes accessed | tf_op | source)
XLA Modules:
  0.0 258.2 jit_solution(4479006054280916460)
XLA Ops:
  7.2 0.0 copy-start
  7.2 0.0 reduce-scatter.7.cloned.1.call-start
  7.2 2.0 convolution_convert_fusion.2
  9.2 0.0 reduce-scatter.7.cloned.1.call-update
  9.3 0.0 all-reduce.3.cloned.1.call-start
  9.3 0.7 copy.10
  10.1 0.1 reduce
  10.2 0.7 sub.3
  10.9 0.0 copy-done
  10.9 1.6 fusion.5
  12.5 0.1 and_convert_fusion
  12.6 3.6 %psum.14 = bf16[24,64]{1,0:T(8,128)(2,1)S(1)} all-reduce(f32[24,64]{1,0:T(8,128)S(1)} %fusion.5), channel_id=1, replica_groups=mesh['grp'=2,'col'=8,'row'=2] {'row'}, use_global_device_ids=true, to_apply=%region_3.0 | all-reduce | flops 1536 | bytes 9216 | tf_op jit(solution)/shard_map/psum | solution.py:24
  16.2 56.6 %reduce-scatter.7.cloned.1.call-done = bf16[24,64]{1,0:T(8,128)(2,1)} async-done(((bf16[192,64]{1,0:T(8,128)(2,1)}), bf16[24,64]{1,0:T(8,128)(2,1)}) %reduce-scatter.7.cloned.1.call-update) | async-done | bytes 3088
  72.8 0.7 convert_element_type.29
  73.5 1.1 convolution_convert_fusion.1
  74.6 0.0 all-reduce.3.cloned.1.call-update
  74.6 0.0 reduce-scatter.5.cloned.1.call-start
  74.7 13.6 %convolution_convert_fusion = bf16[192,13312]{1,0:T(8,128)(2,1)} fusion(bf16[192,1024]{1,0:T(8,128)(2,1)} %param.6, bf16[1024,13312]{1,0:T(8,128)(2,1)} %param.8), kind=kOutput, calls=%fused_computation | convolution fusion | flops 5237047296 | bytes 32768000 | tf_op jit(solution)/shard_map/dot_general | solution.py:26
  88.2 0.0 reduce-scatter.5.cloned.1.call-update
  88.2 58.1 %all-reduce.3.cloned.1.call-done = bf16[16,64,64]{2,1,0:T(8,128)(2,1)} async-done(((bf16[16,64,64]{2,1,0:T(8,128)(2,1)}), bf16[16,64,64]{2,1,0:T(8,128)(2,1)}) %all-reduce.3.cloned.1.call-update) | async-done | bytes 131088 | tf_op jit(solution)/shard_map/psum | solution.py:37
  146.3 1.8 convert_element_type.32
  148.1 103.6 %reduce-scatter.5.cloned.1.call-done = bf16[24,13312]{1,0:T(8,128)(2,1)} async-done(((bf16[192,13312]{1,0:T(8,128)(2,1)}), bf16[24,13312]{1,0:T(8,128)(2,1)}) %reduce-scatter.5.cloned.1.call-update) | async-done | bytes 638992 | tf_op jit(solution)/shard_map/reduce_scatter | solution.py:25
  (2 shorter events, 0.0 us)
Async XLA Ops:
  7.2 3.7 %copy-start = (bf16[64,13312]{1,0:T(8,128)(2,1)S(1)}, bf16[64,13312]{1,0:T(8,128)(2,1)}, u32[]{:S(2)}) copy-start(bf16[64,13312]{1,0:T(8,128)(2,1)} %param.9) | copy-start | bytes 5111812
  7.2 65.6 %reduce-scatter.7.cloned.1.call-start = ((), (), s32[]{:S(2)}) async-start(), calls=%async_computation.4 | async-start | bytes 55296
  9.3 137.1 %all-reduce.3.cloned.1.call-start = ((), (), s32[]{:S(2)}) async-start(), calls=%async_computation.3 | async-start | bytes 524288 | tf_op jit(solution)/shard_map/psum | solution.py:37
  74.6 177.1 %reduce-scatter.5.cloned.1.call-start = ((), (), s32[]{:S(2)}) async-start(), calls=%async_computation.2 | async-start | bytes 5750784 | tf_op jit(solution)/shard_map/reduce_scatter | solution.py:25
Sparse Core Ops, SparseCore 0:
  12.0 60.7 reduce-scatter.6
  76.7 69.5 all-reduce.2
  151.1 100.5 reduce-scatter.4
where the time goes:
time: 258 us
  waiting for transfers between devices  218 us (84%)
  matrix products  18.3 us (7%)
  between operations  13.8 us (5%)
  blocking collectives  3.58 us (1%)
  other arithmetic  3.39 us (1%)
    reduce_scatter x1, waiting for transfers between devices, local(): lax.psum_scatter(jnp.dot(grad_out, weight, preferred_element_type=jnp.flo...  104 us
    psum x1, waiting for transfers between devices, local(): lax.psum(local_docs.astype(jnp.bfloat16), 'col').astype(jnp.float32)  58.1 us
    unnamed x4, waiting for transfers between devices  56.6 us
    dot_general x1, matrix products, local(): jnp.dot(grad_out, weight, preferred_element_type=jnp.float32)  13.6 us
  transfers between devices with their start and end apart: 3, of which 3 were waited for; matrix products, arithmetic and copies ran while one was open for 7% of the time, Pallas kernels for 0%

commit v1 on v0

--- a/solution.py
+++ b/solution.py
@@ -1,7 +1,15 @@
+import functools
+
 import jax
 import jax.numpy as jnp
 from jax import lax
+from jax.experimental import pallas as pl
+from jax.experimental.pallas import tpu as pltpu
 from jax.sharding import PartitionSpec as P
+
+MESH = pl.DeviceIdType.MESH
+F32, BF16 = jnp.float32, jnp.bfloat16
+NT_DIMS = (((1,), (1,)), ((), ()))
 
 
 def member_table(doc_len, first, count):
@@ -38,6 +46,382 @@
     return (input_grad, doc_grads)
 
 
+def add(a, b):
+    return (a.astype(F32) + b.astype(F32)).astype(BF16)
+
+
+def kernel(
+    T, nt, nzt, wbufs,
+    doc_ref, grad_hbm, hid_hbm, w_hbm, pin_hbm, pout_hbm,
+    og_ref, docs_ref,
+    gp, gf, gb, hid, pin, pout, wb,
+    S, Q, YR, RR, RL, FO, FS, FR,
+    SK, SKR, ISK, ISR, G,
+    ld_sem, w_sem,
+    y_s, y_r, zr_s, zr_r, zl_s, zl_r, f_s, f_r,
+    sk_s, sk_r, is_sem, g_s, g_r,
+):
+    nz, ny = 2 * nzt, nt - nzt
+    nu = nz + ny
+    half = T // 2
+    rows = gp.shape[1]
+    kr = pout.shape[0]
+    ff = hid.shape[1]
+
+    c = lax.axis_index("col")
+    r = lax.axis_index("row")
+    y, z = lax.rem(c, 2), lax.div(c, 2)
+    other = c + 1 - 2 * y
+    right, left = lax.rem(c + 2, 8), lax.rem(c + 6, 8)
+
+    def dest(i):
+        return 2 * (i % 4) + (y if i < 4 else 1 - y)
+
+    grad_in = [pltpu.make_async_copy(grad_hbm.at[dest(i)], gp.at[i], ld_sem.at[i]) for i in range(8)]
+    for cp in grad_in:
+        cp.start()
+
+    def w_copy(t):
+        return pltpu.make_async_copy(
+            w_hbm.at[:, pl.ds(pl.multiple_of(t * T, T), T)], wb.at[lax.rem(t, wbufs)], w_sem.at[lax.rem(t, wbufs)]
+        )
+
+    w_copy(jnp.int32(0)).start()
+    pout_in = pltpu.make_async_copy(pout_hbm, pout, ld_sem.at[8])
+    pin_in = pltpu.make_async_copy(pin_hbm, pin, ld_sem.at[9])
+    hid_in = pltpu.make_async_copy(hid_hbm, hid, ld_sem.at[10])
+    for t in range(1, wbufs):
+        w_copy(jnp.int32(t)).start()
+    pout_in.start()
+    hid_in.start()
+    pin_in.start()
+
+    barrier = pltpu.get_barrier_semaphore()
+    for d in range(1, 8):
+        pl.semaphore_signal(barrier, inc=1, device_id={"col": lax.rem(c + d, 8)}, device_id_type=MESH)
+    pl.semaphore_signal(barrier, inc=1, device_id={"row": 1 - r}, device_id_type=MESH)
+
+    def remote(src, dst, s, rcv, to):
+        return pltpu.make_async_remote_copy(
+            src_ref=src, dst_ref=dst, send_sem=s, recv_sem=rcv, device_id=to, device_id_type=MESH
+        )
+
+    def y_copy(k):
+        return remote(Q.at[k], YR.at[k], y_s.at[k], y_r.at[k], {"col": other})
+
+    def zr_copy(u, lo):
+        return remote(S.at[u, lo:4], RR.at[u, lo - 1 : 3], zr_s.at[u], zr_r.at[u], {"col": right})
+
+    def zl_copy(u, hi):
+        return remote(S.at[u, 0:hi], RL.at[u, 0:hi], zl_s.at[u], zl_r.at[u], {"col": left})
+
+    def f_copy(u):
+        return remote(FS.at[u], FR.at[u], f_s.at[u], f_r.at[u], {"col": other})
+
+    def end_sends(u):
+        @pl.when(z == 0)
+        def _():
+            zr_copy(u, 1).start()
+
+        @pl.when(z == 3)
+        def _():
+            zl_copy(u, 3).start()
+
+    for cp in grad_in:
+        cp.wait()
+    for i in range(8):
+        gf[rows * i : rows * (i + 1), :] = gp[i].astype(F32)
+    gb[...] = gf[...].astype(BF16)
+
+    def product(slot, at):
+        return jnp.dot(gb[...], wb[slot, :, at : at + half], preferred_element_type=F32)
+
+    def refill(t):
+        @pl.when(t + wbufs < nt)
+        def _():
+            w_copy(t + wbufs).start()
+
+    def y_tile(t):
+        k = jnp.where(t == 0, 0, t - nzt)
+        w_copy(t).wait()
+        slot = lax.rem(t, wbufs)
+        for n in range(2):
+            got = product(slot, n * half)
+            for b in range(4):
+                S[nz + k, b, :, n * half : (n + 1) * half] = got[rows * b : rows * (b + 1)].astype(BF16)
+                Q[k, b, :, n * half : (n + 1) * half] = got[rows * (b + 4) : rows * (b + 5)].astype(BF16)
+        refill(t)
+        y_copy(k).start()
+
+    def z_tile(t):
+        w_copy(t).wait()
+        slot = lax.rem(t, wbufs)
+        for n in range(2):
+            u = 2 * (t - 1) + n
+            got = product(slot, n * half)
+            for b in range(4):
+                S[u, b, :, 0:half] = got[rows * b : rows * (b + 1)].astype(BF16)
+                S[u, b, :, half:T] = got[rows * (b + 4) : rows * (b + 5)].astype(BF16)
+            end_sends(u)
+        refill(t)
+
+    def over(first, last, body):
+        def step(i, carry):
+            body(i)
+            return carry
+
+        lax.fori_loop(first, last, step, 0)
+
+    pl.semaphore_wait(barrier, 8)
+
+    over(0, 1, y_tile)
+    over(1, 1 + nzt, z_tile)
+
+    def sk_copy(i):
+        return remote(SK.at[i], SKR.at[c], sk_s.at[i], sk_r.at[c], {"col": dest(i)})
+
+    def sk_arrival(j):
+        return remote(SK.at[0], SKR.at[j], sk_s.at[0], sk_r.at[j], {"col": other})
+
+    is_copy = remote(ISK, ISR, is_sem.at[0], is_sem.at[1], {"row": 1 - r})
+
+    def g_copy(d):
+        return remote(G.at[c], G.at[c], g_s.at[d - 1], g_r.at[c], {"col": lax.rem(c + d, 8)})
+
+    def g_arrival(j):
+        return remote(G.at[j], G.at[j], g_s.at[0], g_r.at[j], {"col": other})
+
+    pout_in.wait()
+    sketch = lax.dot_general(gb[...], pout[...], NT_DIMS, preferred_element_type=F32)
+    blank = jnp.zeros((rows, 128 - kr), F32)
+    for i in range(8):
+        SK[i] = jnp.concatenate([sketch[rows * i : rows * (i + 1)], blank], axis=1).astype(BF16)
+        if i < 4:
+            @pl.when(z != i)
+            def _():
+                sk_copy(i).start()
+        else:
+            sk_copy(i).start()
+    hid_in.wait()
+    pin_in.wait()
+    part = jnp.zeros((rows, kr), F32)
+    for k in range(ff // T):
+        part += lax.dot_general(
+            hid[:, k * T : (k + 1) * T], pin[:, k * T : (k + 1) * T], NT_DIMS, preferred_element_type=F32
+        )
+    ISK[...] = jnp.concatenate([blank, part], axis=1)
+    is_copy.start()
+
+    over(1 + nzt, nt, y_tile)
+
+    total = SK[z].astype(F32)
+    for d in range(1, 8):
+        j = lax.rem(c + d, 8)
+        sk_arrival(j).wait_recv()
+        total += SKR[j].astype(F32)
+    is_copy.wait_recv()
+    G[c] = (total + (ISK[...] + ISR[...])).astype(BF16)
+    for d in range(1, 8):
+        g_copy(d).start()
+
+    def y_stage(u):
+        k = u - nz
+        y_copy(k).wait_recv()
+        for b in range(4):
+            S[u, b] = add(S[u, b], YR[k, b])
+        end_sends(u)
+
+    def second(u):
+        @pl.when(z == 1)
+        def _():
+            zr_copy(u, 1).wait_recv()
+            for b in (2, 3):
+                S[u, b] = add(S[u, b], RR[u, b - 1])
+            zr_copy(u, 2).start()
+
+        @pl.when(z == 2)
+        def _():
+            zl_copy(u, 3).wait_recv()
+            for b in (0, 1):
+                S[u, b] = add(S[u, b], RL[u, b])
+            zl_copy(u, 2).start()
+
+    def third(u):
+        @pl.when(z == 2)
+        def _():
+            zr_copy(u, 2).wait_recv()
+            S[u, 3] = add(S[u, 3], RR[u, 2])
+            zr_copy(u, 3).start()
+
+        @pl.when(z == 1)
+        def _():
+            zl_copy(u, 2).wait_recv()
+            S[u, 0] = add(S[u, 0], RL[u, 0])
+            zl_copy(u, 1).start()
+
+    def store(u, value):
+        @pl.when(u < nz)
+        def _():
+            FO[u] = value[:, 0:half].astype(BF16)
+            FS[u] = value[:, half:T].astype(BF16)
+            f_copy(u).start()
+
+        @pl.when(u >= nz)
+        def _():
+            k = u - nz
+            t = jnp.where(k == 0, 0, k + nzt)
+            og_ref[:, pl.ds(pl.multiple_of(t * T, T), T)] = value.astype(BF16)
+
+    def last(u):
+        @pl.when(z == 0)
+        def _():
+            zl_copy(u, 1).wait_recv()
+            store(u, S[u, 0].astype(F32) + RL[u, 0].astype(F32))
+
+        @pl.when(z == 3)
+        def _():
+            zr_copy(u, 3).wait_recv()
+            store(u, S[u, 3].astype(F32) + RR[u, 2].astype(F32))
+
+        @pl.when(z == 1)
+        def _():
+            store(u, S[u, 1].astype(F32) + RR[u, 0].astype(F32) + RL[u, 1].astype(F32))
+
+        @pl.when(z == 2)
+        def _():
+            store(u, S[u, 2].astype(F32) + RR[u, 1].astype(F32) + RL[u, 2].astype(F32))
+
+    def fold(u):
+        f_copy(u).wait_recv()
+        og_ref[:, pl.ds(pl.multiple_of(T + u * half, half), half)] = add(FO[u], FR[u])
+
+    def step(i):
+        @pl.when((i >= nz) & (i < nu))
+        def _():
+            y_stage(i)
+
+        @pl.when((i >= 1) & (i < nu + 1))
+        def _():
+            second(i - 1)
+
+        @pl.when((i >= 2) & (i < nu + 2))
+        def _():
+            third(i - 2)
+
+        @pl.when((i >= 3) & (i < nu + 3))
+        def _():
+            last(i - 3)
+
+        @pl.when((i >= 5) & (i < nz + 5))
+        def _():
+            fold(i - 5)
+
+    over(0, nz + 5, step)
+
+    for d in range(1, 8):
+        g_arrival(lax.rem(c + d, 8)).wait_recv()
+    both = jnp.concatenate([G[j].astype(F32) for j in range(8)], axis=0).astype(BF16)
+    eye = (
+        lax.broadcasted_iota(jnp.int32, (kr, 128), 0) == lax.broadcasted_iota(jnp.int32, (kr, 128), 1)
+    ).astype(F32).astype(BF16)
+    turned = lax.dot_general(eye, both, NT_DIMS, preferred_element_type=F32)
+    place = lax.broadcasted_iota(jnp.int32, turned.shape, 1)
+    start = jnp.int32(0)
+    for s in range(docs_ref.shape[0]):
+        stop = start + doc_ref[s]
+        mine = jnp.where((place >= start) & (place < stop), turned, 0.0).astype(BF16)
+        docs_ref[s] = jnp.dot(mine, both, preferred_element_type=F32)[:, kr : 2 * kr]
+        start = stop
+
+    over(nz + 5, nu + 3, step)
+
+    def sent_y(k):
+        y_copy(k).wait_send()
+
+    def sent_f(u):
+        f_copy(u).wait_send()
+
+    def sent_z(u):
+        for at in range(4):
+            @pl.when(z == at)
+            def _():
+                if at < 3:
+                    zr_copy(u, at + 1).wait_send()
+                if at > 0:
+                    zl_copy(u, at).wait_send()
+
+    over(0, ny, sent_y)
+    over(0, nz, sent_f)
+    over(0, nu, sent_z)
+    for i in range(8):
+        if i < 4:
+            @pl.when(z != i)
+            def _():
+                sk_copy(i).wait_send()
+        else:
+            sk_copy(i).wait_send()
+    is_copy.wait_send()
+    for d in range(1, 8):
+        g_copy(d).wait_send()
+
+
+def fused(grad_out, hidden, weight, proj_in, proj_out, doc_len, T=512, wbufs=4):
+    tokens, depth = grad_out.shape
+    rows, ff = hidden.shape
+    kr = proj_in.shape[0]
+    docs = doc_len.shape[0]
+    nt = ff // T
+    nzt = max(1, (2 * nt + 6) // 13)
+    nz, ny = 2 * nzt, nt - nzt
+    nu = nz + ny
+    dma = pltpu.SemaphoreType.DMA
+    any_spec = pl.BlockSpec(memory_space=pl.ANY)
+    vmem_spec = pl.BlockSpec(memory_space=pltpu.VMEM)
+    return pl.pallas_call(
+        functools.partial(kernel, T, nt, nzt, wbufs),
+        out_shape=(
+            jax.ShapeDtypeStruct((rows, ff), BF16),
+            jax.ShapeDtypeStruct((docs, kr, kr), F32),
+        ),
+        in_specs=[pl.BlockSpec(memory_space=pltpu.SMEM)] + [any_spec] * 5,
+        out_specs=(vmem_spec, vmem_spec),
+        scratch_shapes=[
+            pltpu.VMEM((8, rows, depth), BF16),
+            pltpu.VMEM((tokens, depth), F32),
+            pltpu.VMEM((tokens, depth), BF16),
+            pltpu.VMEM((rows, ff), BF16),
+            pltpu.VMEM((kr, ff), BF16),
+            pltpu.VMEM((kr, depth), BF16),
+            pltpu.VMEM((wbufs, depth, T), BF16),
+            pltpu.VMEM((nu, 4, rows, T), BF16),
+            pltpu.VMEM((ny, 4, rows, T), BF16),
+            pltpu.VMEM((ny, 4, rows, T), BF16),
+            pltpu.VMEM((nu, 3, rows, T), BF16),
+            pltpu.VMEM((nu, 3, rows, T), BF16),
+            pltpu.VMEM((nz, rows, T // 2), BF16),
+            pltpu.VMEM((nz, rows, T // 2), BF16),
+            pltpu.VMEM((nz, rows, T // 2), BF16),
+            pltpu.VMEM((8, rows, 128), BF16),
+            pltpu.VMEM((8, rows, 128), BF16),
+            pltpu.VMEM((rows, 128), F32),
+            pltpu.VMEM((rows, 128), F32),
+            pltpu.VMEM((8, rows, 128), BF16),
+            dma((11,)),
+            dma((wbufs,)),
+            dma((ny,)), dma((ny,)),
+            dma((nu,)), dma((nu,)), dma((nu,)), dma((nu,)),
+            dma((nz,)), dma((nz,)),
+            dma((8,)), dma((8,)), dma((2,)), dma((7,)), dma((8,)),
+        ],
+        compiler_params=pltpu.CompilerParams(
+            collective_id=0, has_side_effects=True, vmem_limit_bytes=48 * 1024 * 1024
+        ),
+        cost_estimate=pl.CostEstimate(
+            flops=2 * tokens * depth * ff, bytes_accessed=2 * depth * ff, transcendentals=0
+        ),
+    )(doc_len, grad_out.reshape(8, rows, depth), hidden, weight, proj_in, proj_out)
+
+
 def solution(mesh):
     in_specs = (
         P("grp", "col"),
@@ -48,4 +432,5 @@
         P("grp"),
     )
     out_specs = (P(("grp", "col"), "row"), P("grp", None, None))
-    return jax.shard_map(local, mesh=mesh, in_specs=in_specs, out_specs=out_specs, check_vma=False)
+    body = fused if mesh.shape["col"] == 8 and mesh.shape["row"] == 2 else local
+    return jax.shard_map(body, mesh=mesh, in_specs=in_specs, out_specs=out_specs, check_vma=False)

time: 258 us -> 133 us (0.52)
  waiting for transfers between devices: 218 us -> 0 us
  Pallas kernels: 0 us -> 126 us
  matrix products: 18.3 us -> 0 us
  between operations: 13.8 us -> 0.65 us
  local copies, waits for them, and re-layouts: 0.74 us -> 6.71 us
  blocking collectives: 3.58 us -> 0 us
  other arithmetic: 3.39 us -> 0 us
    pallas_call x0 -> x1, Pallas kernels: none -> 126 us  [fused(): pl.pallas_call(functools.partial(kernel, T, nt, nzt, wbufs), out_shape=(j...]
    reduce_scatter x1 -> x0, waiting for transfers between devices: 104 us -> none  [local(): lax.psum_scatter(jnp.dot(grad_out, weight, preferred_element_type=jnp.flo...]
    psum x1 -> x0, waiting for transfers between devices: 58.1 us -> none  [local(): lax.psum(local_docs.astype(jnp.bfloat16), 'col').astype(jnp.float32)]
    unnamed x4 -> x0, waiting for transfers between devices: 56.6 us -> none
    dot_general x4 -> x0, matrix products: 18.3 us -> none  [the longest x1 13.6 us: local(): jnp.dot(grad_out, weight, preferred_element_type=jnp.float32)]
    unnamed x2 -> x12, local copies, waits for them, and re-layouts: 0.01 us -> 6.71 us
    psum x1 -> x0, blocking collectives: 3.58 us -> none  [local(): in_sketch = lax.psum(local_in, 'row').astype(jnp.bfloat16)]
  transfers between devices with their start and end apart: 3 -> 0, of which waited for: 3 -> 0; matrix products, arithmetic and copies ran while one was open for 7% -> 0% of each run, Pallas kernels for 0% -> 0%
where the time goes in v1:
time: 133 us
  Pallas kernels  126 us (95%)
  local copies, waits for them, and re-layouts  6.71 us (5%)
    pallas_call x1, Pallas kernels, fused(): pl.pallas_call(functools.partial(kernel, T, nt, nzt, wbufs), out_shape=(j...  126 us
    unnamed x12, local copies, waits for them, and re-layouts  6.71 us

profile of v1, /device:TPU:0, one launch (start us, length us, event | category | flops | bytes accessed | tf_op | source)
XLA Modules:
  0.0 133.2 jit_solution(999353108765629999)
XLA Ops:
  0.6 0.0 copy-start
  0.6 1.4 %copy-done = bf16[64,13312]{1,0:T(8,128)(2,1)S(1)} copy-done((bf16[64,13312]{1,0:T(8,128)(2,1)S(1)}, bf16[64,13312]{1,0:T(8,128)(2,1)}, u32[]{:S(2)}) %copy-start) | copy-done | bytes 1703960
  2.1 0.0 copy-start.1
  2.1 1.1 copy-done.1
  3.2 0.0 copy-start.2
  3.2 1.0 copy-done.2
  4.2 0.0 copy-start.3
  4.2 0.9 copy-done.3
  5.1 0.0 copy-start.4
  5.1 0.7 copy-done.4
  5.7 125.8 %shard_map.77 = (bf16[24,13312]{1,0:T(8,128)(2,1)S(1)}, f32[16,64,64]{2,1,0:T(8,128)S(1)}) custom-call(s32[16]{0:T(128)S(1)} %copy-done.4, bf16[8,24,1024]{2,1,0:T(8,128)(2,1)S(1)} %bitcast.1, bf16[24,13312]{1,0:T(8,128)(2,1)S(1)} %copy-done.1, bf16[1024,13312]{1,0:T(8,128)(2,1)} %w_hbm.1, bf16[64,13312]{1,0:T(8,128)(2,1)S(1)} %copy-done, ...), custom_call_target="tpu_custom_call" | custom-call | flops 5234491392 | bytes 27262976 | tf_op jit(solution)/shard_map/pallas_call | solution.py:380
  131.6 0.8 copy.10
  132.4 0.8 copy.11
Async XLA Ops:
  0.6 1.5 %copy-start = (bf16[64,13312]{1,0:T(8,128)(2,1)S(1)}, bf16[64,13312]{1,0:T(8,128)(2,1)}, u32[]{:S(2)}) copy-start(bf16[64,13312]{1,0:T(8,128)(2,1)} %pin_hbm.1) | copy-start | bytes 5111812
  2.1 1.1 copy-start.1
  3.2 1.0 copy-start.2
  4.2 0.9 copy-start.3
  5.1 0.7 copy-start.4

commit v2 on v1

--- a/solution.py
+++ b/solution.py
@@ -51,7 +51,7 @@
 
 
 def kernel(
-    T, nt, nzt, wbufs,
+    T, nt, nzt, wbufs, lag,
     doc_ref, grad_hbm, hid_hbm, w_hbm, pin_hbm, pout_hbm,
     og_ref, docs_ref,
     gp, gf, gb, hid, pin, pout, wb,
@@ -63,6 +63,7 @@
 ):
     nz, ny = 2 * nzt, nt - nzt
     nu = nz + ny
+    early = min(3 + nzt, nt)
     half = T // 2
     rows = gp.shape[1]
     kr = pout.shape[0]
@@ -174,9 +175,6 @@
 
     pl.semaphore_wait(barrier, 8)
 
-    over(0, 1, y_tile)
-    over(1, 1 + nzt, z_tile)
-
     def sk_copy(i):
         return remote(SK.at[i], SKR.at[c], sk_s.at[i], sk_r.at[c], {"col": dest(i)})
 
@@ -202,6 +200,9 @@
                 sk_copy(i).start()
         else:
             sk_copy(i).start()
+    over(0, 1, y_tile)
+    over(1, 1 + nzt, z_tile)
+
     hid_in.wait()
     pin_in.wait()
     part = jnp.zeros((rows, kr), F32)
@@ -212,7 +213,7 @@
     ISK[...] = jnp.concatenate([blank, part], axis=1)
     is_copy.start()
 
-    over(1 + nzt, nt, y_tile)
+    over(1 + nzt, early, y_tile)
 
     total = SK[z].astype(F32)
     for d in range(1, 8):
@@ -224,99 +225,7 @@
     for d in range(1, 8):
         g_copy(d).start()
 
-    def y_stage(u):
-        k = u - nz
-        y_copy(k).wait_recv()
-        for b in range(4):
-            S[u, b] = add(S[u, b], YR[k, b])
-        end_sends(u)
-
-    def second(u):
-        @pl.when(z == 1)
-        def _():
-            zr_copy(u, 1).wait_recv()
-            for b in (2, 3):
-                S[u, b] = add(S[u, b], RR[u, b - 1])
-            zr_copy(u, 2).start()
-
-        @pl.when(z == 2)
-        def _():
-            zl_copy(u, 3).wait_recv()
-            for b in (0, 1):
-                S[u, b] = add(S[u, b], RL[u, b])
-            zl_copy(u, 2).start()
-
-    def third(u):
-        @pl.when(z == 2)
-        def _():
-            zr_copy(u, 2).wait_recv()
-            S[u, 3] = add(S[u, 3], RR[u, 2])
-            zr_copy(u, 3).start()
-
-        @pl.when(z == 1)
-        def _():
-            zl_copy(u, 2).wait_recv()
-            S[u, 0] = add(S[u, 0], RL[u, 0])
-            zl_copy(u, 1).start()
-
-    def store(u, value):
-        @pl.when(u < nz)
-        def _():
-            FO[u] = value[:, 0:half].astype(BF16)
-            FS[u] = value[:, half:T].astype(BF16)
-            f_copy(u).start()
-
-        @pl.when(u >= nz)
-        def _():
-            k = u - nz
-            t = jnp.where(k == 0, 0, k + nzt)
-            og_ref[:, pl.ds(pl.multiple_of(t * T, T), T)] = value.astype(BF16)
-
-    def last(u):
-        @pl.when(z == 0)
-        def _():
-            zl_copy(u, 1).wait_recv()
-            store(u, S[u, 0].astype(F32) + RL[u, 0].astype(F32))
-
-        @pl.when(z == 3)
-        def _():
-            zr_copy(u, 3).wait_recv()
-            store(u, S[u, 3].astype(F32) + RR[u, 2].astype(F32))
-
-        @pl.when(z == 1)
-        def _():
-            store(u, S[u, 1].astype(F32) + RR[u, 0].astype(F32) + RL[u, 1].astype(F32))
-
-        @pl.when(z == 2)
-        def _():
-            store(u, S[u, 2].astype(F32) + RR[u, 1].astype(F32) + RL[u, 2].astype(F32))
-
-    def fold(u):
-        f_copy(u).wait_recv()
-        og_ref[:, pl.ds(pl.multiple_of(T + u * half, half), half)] = add(FO[u], FR[u])
-
-    def step(i):
-        @pl.when((i >= nz) & (i < nu))
-        def _():
-            y_stage(i)
-
-        @pl.when((i >= 1) & (i < nu + 1))
-        def _():
-            second(i - 1)
-
-        @pl.when((i >= 2) & (i < nu + 2))
-        def _():
-            third(i - 2)
-
-        @pl.when((i >= 3) & (i < nu + 3))
-        def _():
-            last(i - 3)
-
-        @pl.when((i >= 5) & (i < nz + 5))
-        def _():
-            fold(i - 5)
-
-    over(0, nz + 5, step)
+    over(early, nt, y_tile)
 
     for d in range(1, 8):
         g_arrival(lax.rem(c + d, 8)).wait_recv()
@@ -333,7 +242,95 @@
         docs_ref[s] = jnp.dot(mine, both, preferred_element_type=F32)[:, kr : 2 * kr]
         start = stop
 
-    over(nz + 5, nu + 3, step)
+    def y_stage(u):
+        k = u - nz
+        y_copy(k).wait_recv()
+        for b in range(4):
+            S[u, b] = add(S[u, b], YR[k, b])
+        end_sends(u)
+
+    def second(u):
+        @pl.when(z == 1)
+        def _():
+            zr_copy(u, 1).wait_recv()
+            for b in (2, 3):
+                S[u, b] = add(S[u, b], RR[u, b - 1])
+            zr_copy(u, 2).start()
+
+        @pl.when(z == 2)
+        def _():
+            zl_copy(u, 3).wait_recv()
+            for b in (0, 1):
+                S[u, b] = add(S[u, b], RL[u, b])
+            zl_copy(u, 2).start()
+
+    def third(u):
+        @pl.when(z == 2)
+        def _():
+            zr_copy(u, 2).wait_recv()
+            S[u, 3] = add(S[u, 3], RR[u, 2])
+            zr_copy(u, 3).start()
+
+        @pl.when(z == 1)
+        def _():
+            zl_copy(u, 2).wait_recv()
+            S[u, 0] = add(S[u, 0], RL[u, 0])
+            zl_copy(u, 1).start()
+
+    def store(u, value):
+        @pl.when(u < nz)
+        def _():
+            FO[u] = value[:, 0:half].astype(BF16)
+            FS[u] = value[:, half:T].astype(BF16)
+            f_copy(u).start()
+
+        @pl.when(u >= nz)
+        def _():
+            k = u - nz
+            t = jnp.where(k == 0, 0, k + nzt)
+            og_ref[:, pl.ds(pl.multiple_of(t * T, T), T)] = value.astype(BF16)
+
+    def last(u):
+        @pl.when(z == 0)
+        def _():
+            zl_copy(u, 1).wait_recv()
+            store(u, S[u, 0].astype(F32) + RL[u, 0].astype(F32))
+
+        @pl.when(z == 3)
+        def _():
+            zr_copy(u, 3).wait_recv()
+            store(u, S[u, 3].astype(F32) + RR[u, 2].astype(F32))
+
+        @pl.when(z == 1)
+        def _():
+            store(u, S[u, 1].astype(F32) + RR[u, 0].astype(F32) + RL[u, 1].astype(F32))
+
+        @pl.when(z == 2)
+        def _():
+            store(u, S[u, 2].astype(F32) + RR[u, 1].astype(F32) + RL[u, 2].astype(F32))
+
+    def fold(u):
+        f_copy(u).wait_recv()
+        og_ref[:, pl.ds(pl.multiple_of(T + u * half, half), half)] = add(FO[u], FR[u])
+
+    def at_lag(i, stages, body):
+        u = i - stages * lag
+
+        @pl.when((u >= 0) & (u < nu))
+        def _():
+            body(u)
+
+    def step(i):
+        @pl.when((i >= nz) & (i < nu))
+        def _():
+            y_stage(i)
+
+        at_lag(i, 1, second)
+        at_lag(i, 2, third)
+        at_lag(i, 3, last)
+
+    over(0, nu + 3 * lag, step)
+    over(0, nz, fold)
 
     def sent_y(k):
         y_copy(k).wait_send()
@@ -365,7 +362,7 @@
         g_copy(d).wait_send()
 
 
-def fused(grad_out, hidden, weight, proj_in, proj_out, doc_len, T=512, wbufs=4):
+def fused(grad_out, hidden, weight, proj_in, proj_out, doc_len, T=512, wbufs=4, lag=3):
     tokens, depth = grad_out.shape
     rows, ff = hidden.shape
     kr = proj_in.shape[0]
@@ -378,7 +375,7 @@
     any_spec = pl.BlockSpec(memory_space=pl.ANY)
     vmem_spec = pl.BlockSpec(memory_space=pltpu.VMEM)
     return pl.pallas_call(
-        functools.partial(kernel, T, nt, nzt, wbufs),
+        functools.partial(kernel, T, nt, nzt, wbufs, lag),
         out_shape=(
             jax.ShapeDtypeStruct((rows, ff), BF16),
             jax.ShapeDtypeStruct((docs, kr, kr), F32),
@@ -414,7 +411,7 @@
             dma((8,)), dma((8,)), dma((2,)), dma((7,)), dma((8,)),
         ],
         compiler_params=pltpu.CompilerParams(
-            collective_id=0, has_side_effects=True, vmem_limit_bytes=48 * 1024 * 1024
+            collective_id=0, has_side_effects=True, vmem_limit_bytes=60 * 1024 * 1024
         ),
         cost_estimate=pl.CostEstimate(
             flops=2 * tokens * depth * ff, bytes_accessed=2 * depth * ff, transcendentals=0

time: 133 us -> 75.9 us (0.57)
  Pallas kernels: 126 us -> 71.1 us
  local copies, waits for them, and re-layouts: 6.71 us -> 3.84 us
    pallas_call x1, Pallas kernels: 126 us -> 71.1 us  [fused(): pl.pallas_call(functools.partial(kernel, T, nt, nzt, wbufs, lag), out_sha...]
    unnamed x12 -> x2, local copies, waits for them, and re-layouts: 6.71 us -> 3.84 us
where the time goes in v2:
time: 75.9 us; the launch traced here: 75.6 us
  Pallas kernels  71.1 us (94%)
  local copies, waits for them, and re-layouts  3.84 us (5%)
    pallas_call x1, Pallas kernels, fused(): pl.pallas_call(functools.partial(kernel, T, nt, nzt, wbufs, lag), out_sha...  71.1 us
    unnamed x2, local copies, waits for them, and re-layouts  3.84 us

profile of v2, /device:TPU:0, one launch (start us, length us, event | category | flops | bytes accessed | tf_op | source)
XLA Modules:
  0.0 75.6 jit_solution(1378483647813897590)
XLA Ops:
  0.6 71.1 %shard_map.77 = (bf16[24,13312]{1,0:T(8,128)(2,1)}, f32[16,64,64]{2,1,0:T(8,128)}) custom-call(s32[16]{0:T(128)} %doc_ref.1, bf16[8,24,1024]{2,1,0:T(8,128)(2,1)} %bitcast.1, bf16[24,13312]{1,0:T(8,128)(2,1)} %hid_hbm.1, bf16[1024,13312]{1,0:T(8,128)(2,1)} %w_hbm.1, bf16[64,13312]{1,0:T(8,128)(2,1)} %pin_hbm.1, bf16[64,1024]{1,0:T(8,128)(2,1)} %pout_hbm.1), custom_call_target="tpu_custom_call" | custom-call | flops 5234491392 | bytes 27262976 | tf_op jit(solution)/shard_map/pallas_call | solution.py:377
  71.8 2.0 %copy.10 = bf16[24,13312]{1,0:T(8,128)(2,1)} copy(bf16[24,13312]{1,0:T(8,128)(2,1)} %get-tuple-element.4) | data formatting | bytes 1277952
  73.7 1.9 %copy.11 = f32[16,64,64]{2,1,0:T(8,128)} copy(f32[16,64,64]{2,1,0:T(8,128)} %get-tuple-element.5) | data formatting | bytes 524288

commit v3 on v2

--- a/solution.py
+++ b/solution.py
@@ -362,6 +362,15 @@
         g_copy(d).wait_send()
 
 
+def settle(a, b, a_out, b_out, sem):
+    first = pltpu.make_async_copy(a, a_out, sem.at[0])
+    second = pltpu.make_async_copy(b, b_out, sem.at[1])
+    first.start()
+    second.start()
+    first.wait()
+    second.wait()
+
+
 def fused(grad_out, hidden, weight, proj_in, proj_out, doc_len, T=512, wbufs=4, lag=3):
     tokens, depth = grad_out.shape
     rows, ff = hidden.shape
@@ -374,12 +383,13 @@
     dma = pltpu.SemaphoreType.DMA
     any_spec = pl.BlockSpec(memory_space=pl.ANY)
     vmem_spec = pl.BlockSpec(memory_space=pltpu.VMEM)
-    return pl.pallas_call(
+    shapes = (
+        jax.ShapeDtypeStruct((rows, ff), BF16),
+        jax.ShapeDtypeStruct((docs, kr, kr), F32),
+    )
+    made = pl.pallas_call(
         functools.partial(kernel, T, nt, nzt, wbufs, lag),
-        out_shape=(
-            jax.ShapeDtypeStruct((rows, ff), BF16),
-            jax.ShapeDtypeStruct((docs, kr, kr), F32),
-        ),
+        out_shape=shapes,
         in_specs=[pl.BlockSpec(memory_space=pltpu.SMEM)] + [any_spec] * 5,
         out_specs=(vmem_spec, vmem_spec),
         scratch_shapes=[
@@ -417,6 +427,13 @@
             flops=2 * tokens * depth * ff, bytes_accessed=2 * depth * ff, transcendentals=0
         ),
     )(doc_len, grad_out.reshape(8, rows, depth), hidden, weight, proj_in, proj_out)
+    return pl.pallas_call(
+        settle,
+        out_shape=shapes,
+        in_specs=[vmem_spec] * 2,
+        out_specs=(any_spec, any_spec),
+        scratch_shapes=[dma((2,))],
+    )(*made)
 
 
 def solution(mesh):

time: 75.9 us -> 74.3 us (0.979)
  local copies, waits for them, and re-layouts: 3.84 us -> 0 us
  Pallas kernels: 71.1 us -> 73.5 us
    unnamed x2 -> x0, local copies, waits for them, and re-layouts: 3.84 us -> none
    pallas_call x0 -> x1, Pallas kernels: none -> 2.25 us  [fused(): pl.pallas_call(settle, out_shape=shapes, in_specs=[vmem_spec] * 2, out_sp...]
where the time goes in v3:
time: 74.3 us; the launch traced here: 74.1 us
  Pallas kernels  73.5 us (99%)
    pallas_call x1, Pallas kernels, fused(): pl.pallas_call(functools.partial(kernel, T, nt, nzt, wbufs, lag), out_sha...  71.2 us
    pallas_call x1, Pallas kernels, fused(): pl.pallas_call(settle, out_shape=shapes, in_specs=[vmem_spec] * 2, out_sp...  2.25 us

profile of v3, /device:TPU:0, one launch (start us, length us, event | category | flops | bytes accessed | tf_op | source)
XLA Modules:
  0.0 74.1 jit_solution(2994938792956274553)
XLA Ops:
  0.6 71.2 %shard_map.77 = (bf16[24,13312]{1,0:T(8,128)(2,1)}, f32[16,64,64]{2,1,0:T(8,128)}) custom-call(s32[16]{0:T(128)} %doc_ref.1, bf16[8,24,1024]{2,1,0:T(8,128)(2,1)} %bitcast.1, bf16[24,13312]{1,0:T(8,128)(2,1)} %hid_hbm.1, bf16[1024,13312]{1,0:T(8,128)(2,1)} %w_hbm.1, bf16[64,13312]{1,0:T(8,128)(2,1)} %pin_hbm.1, bf16[64,1024]{1,0:T(8,128)(2,1)} %pout_hbm.1), custom_call_target="tpu_custom_call" | custom-call | flops 5234491392 | bytes 27262976 | tf_op jit(solution)/shard_map/pallas_call | solution.py:390
  71.9 2.3 %shard_map.78 = (bf16[24,13312]{1,0:T(8,128)(2,1)}, f32[16,64,64]{2,1,0:T(8,128)}) custom-call(bf16[24,13312]{1,0:T(8,128)(2,1)} %get-tuple-element.4.a, f32[16,64,64]{2,1,0:T(8,128)} %get-tuple-element.5.b), custom_call_target="tpu_custom_call" | custom-call | tf_op jit(solution)/shard_map/pallas_call | solution.py:430
